TPU v7x, 768 devices: a whole 4x8x12 slice. The times are simulated.
768 devices in a mesh: dp: 12 (over z), emb: 64 (over y, x, core).
Axes of the slice: x: 4, y: 8, z: 12, core: 2. Of those that a mesh axis runs over, the one named last changes fastest.
Arguments:
- emb_table: bfloat16 [65536, 192], P('emb'), may hold values from -6 to 6
- requests: int32 [768, 64, 32], P(('dp', 'emb')), may hold values from 0 to 1023
- token_slot: int32 [768, 2048], P(('dp', 'emb')), may hold values from 0 to 2047, each once within a row
- kept_mask: int32 [6144, 256], P(('dp', 'emb')), may hold values 0 or 1
- fm_proj: bfloat16 [256, 96], replicated, may hold values from -0.375 to 0.375
- comp_weight: bfloat16 [256, 256], replicated, may hold values from -0.375 to 0.375
- comp_cotangent: bfloat16 [6144, 49152], P(('dp', 'emb')), may hold values from -6 to 6
Outputs:
- fm_tokens: bfloat16 [6144, 24576], P(('dp', 'emb'))
- compressed: bfloat16 [6144, 49152], P(('dp', 'emb'))
- table_grad: float32 [65536, 192], P('emb')
- weight_grad: float32 [256, 256], replicated
Inputs may be any that keep to these rules, and one draw needn't show every extreme that they name: Each device's row of token_slot names every slot once.
All inputs are finite; a program needn't handle non-finite values. No bound on the sum of `kept_mask` on one device may be relied on, other than what follows from the above.
Results may differ from a plain program's by a relative error of at most 0.0038.
Values may be sent and summed in bfloat16 or wider, within the bound.
A program may use at most 32 MiB of HBM per device.

v0:
```python
import jax
import jax.numpy as jnp
from jax import lax
from jax.sharding import PartitionSpec as P


def on_device(emb_table, requests, token_slot, kept_mask, fm_proj, comp_weight, comp_cotangent):
    groups = lax.axis_size("emb")
    batch = kept_mask.shape[0]
    ntoken = kept_mask.shape[1]
    width = emb_table.shape[1]
    ncomp = comp_weight.shape[0]
    asked = lax.all_to_all(requests, "emb", split_axis=1, concat_axis=1, tiled=True)
    wanted = asked.reshape(-1)
    fetched = jnp.take(emb_table, wanted, axis=0).reshape(groups, -1, width)
    arrived = lax.all_to_all(fetched, "emb", split_axis=0, concat_axis=0, tiled=True).reshape(
        -1, width
    )
    slots = token_slot.reshape(-1)
    gathered = jnp.take(arrived, slots, axis=0).reshape(batch, ntoken, width)
    embedded = gathered * kept_mask[:, :, None].astype(jnp.bfloat16)
    projected = jnp.einsum(
        "bnd,nk->bdk", embedded, fm_proj, preferred_element_type=jnp.float32
    ).astype(jnp.bfloat16)
    fm_raw = jnp.einsum("bnd,bdk->bnk", embedded, projected, preferred_element_type=jnp.float32)
    mean = jnp.mean(fm_raw, axis=(1, 2), keepdims=True)
    variance = jnp.mean((fm_raw - mean) ** 2, axis=(1, 2), keepdims=True)
    fm_tokens = (
        ((fm_raw - mean) * lax.rsqrt(variance + 1e-05)).astype(jnp.bfloat16).reshape(batch, -1)
    )
    compressed = jnp.einsum(
        "mn,bnd->bmd", comp_weight, embedded, preferred_element_type=jnp.float32
    )
    compressed = compressed.astype(jnp.bfloat16).reshape(batch, -1)
    cotangent = comp_cotangent.reshape(batch, ncomp, width)
    row_grad = jnp.einsum("mn,bmd->bnd", comp_weight, cotangent, preferred_element_type=jnp.float32)
    row_grad = row_grad * kept_mask[:, :, None].astype(jnp.float32)
    weight_local = jnp.einsum(
        "bmd,bnd->mn", cotangent, embedded, preferred_element_type=jnp.float32
    )
    ordered = (
        jnp.zeros((slots.shape[0], width), jnp.float32).at[slots].set(row_grad.reshape(-1, width))
    )
    returned = lax.all_to_all(
        ordered.reshape(groups, -1, width), "emb", split_axis=0, concat_axis=0, tiled=True
    ).reshape(-1, width)
    table_local = jax.ops.segment_sum(returned, wanted, num_segments=emb_table.shape[0])
    table_grad = lax.psum(table_local, "dp")
    weight_total = lax.psum(weight_local, ("dp", "emb"))
    samples_total = batch * lax.axis_size("dp") * groups
    weight_grad = weight_total / jnp.float32(samples_total)
    return (fm_tokens, compressed, table_grad, weight_grad)


def solution(mesh):
    return jax.shard_map(
        on_device,
        mesh=mesh,
        in_specs=(
            P("emb", None),
            P(("dp", "emb"), None, None),
            P(("dp", "emb"), None),
            P(("dp", "emb"), None),
            P(),
            P(),
            P(("dp", "emb"), None),
        ),
        out_specs=(P(("dp", "emb"), None), P(("dp", "emb"), None), P("emb", None), P()),
        check_vma=False,
    )
```

profile of v0, /device:TPU:1, one launch (start us, length us, event | category | flops | bytes accessed | tf_op | source)
XLA Modules:
  0.0 678.7 jit_solution(17104862360309630329)
XLA Ops:
  7.2 1.4 copy.32
  8.6 14.5 %all-to-all-start = ((s32[1,64,32]{2,0,1:T(1,128)}), s32[1,64,32]{2,0,1:T(1,128)S(1)}, u32[]{:S(2)}, u32[]{:S(2)}) async-start(s32[1,64,32]{2,0,1:T(1,128)} %copy.32), calls=%async_computation | async-start | bytes 65536 | tf_op jit(solution)/shard_map/all_to_all | solution.py:13
  23.2 1.2 copy.33
  24.4 8.2 %all-to-all-done = s32[1,64,32]{2,0,1:T(1,128)S(1)} async-done(((s32[1,64,32]{2,0,1:T(1,128)}), s32[1,64,32]{2,0,1:T(1,128)S(1)}, u32[]{:S(2)}, u32[]{:S(2)}) %all-to-all-start) | async-done | bytes 8224 | tf_op jit(solution)/shard_map/all_to_all | solution.py:13
  32.6 0.5 broadcast.153
  33.1 0.7 reduce.8
  34.0 7.5 %gather_fusion = bf16[2048,192]{1,0:T(8,128)(2,1)S(1)} fusion(bf16[1024,192]{1,0:T(8,128)(2,1)S(1)} %copy.33, s32[2048]{0:T(1024)S(1)} %broadcast_clamp_fusion.1), kind=kCustom, calls=%fused_computation | custom fusion | bytes 1581056 | tf_op jit(solution)/shard_map/jit(_take)/gather | solution.py:15
  41.5 1.3 broadcast_select_fusion
  42.7 4.9 all-to-all-start.1
  47.7 1.2 reshape.178
  48.9 1.7 multiply_bitcast_fusion
  50.6 2.8 copy.49
  53.4 10.9 %scatter_custom_fusion = f32[2048,192]{1,0:T(8,128)} fusion(s32[2048]{0:T(1024)S(1)} %bitcast.47, f32[2048,192]{1,0:T(8,128)} %bitcast.44, f32[]{:T(128)} %constant.41.clone.1), kind=kCustom, calls=%fused_computation.11 | custom fusion | bytes 1573376 | tf_op jit(solution)/shard_map/scatter | solution.py:42
  64.3 11.5 %all-to-all-done.1 = bf16[64,32,192]{2,1,0:T(8,128)(2,1)S(1)} async-done(((bf16[64,32,192]{2,1,0:T(8,128)(2,1)}), bf16[64,32,192]{2,1,0:T(8,128)(2,1)S(1)}, u32[]{:S(2)}, u32[]{:S(2)}) %all-to-all-start.1) | async-done | bytes 786464 | tf_op jit(solution)/shard_map/all_to_all | solution.py:16
  75.8 6.6 all-to-all-start.2
  82.5 0.7 reduce.9
  83.3 7.5 %gather_fusion.1 = bf16[2048,192]{1,0:T(8,128)(2,1)S(1)} fusion(bf16[2048,192]{1,0:T(8,128)(2,1)S(1)} %bitcast.39, s32[2048]{0:T(1024)S(1)} %broadcast_clamp_fusion), kind=kCustom, calls=%fused_computation.1 | custom fusion | bytes 1581056 | tf_op jit(solution)/shard_map/jit(_take)/gather | solution.py:20
  90.8 1.3 copy.34
  92.0 0.7 select_multiply_fusion
  92.8 1.2 convolution_bitcast_fusion
  94.2 0.8 fusion.20
  95.3 36.9 %all-to-all-done.2 = f32[64,32,192]{2,1,0:T(8,128)} async-done(((f32[64,32,192]{2,1,0:T(8,128)}), f32[64,32,192]{2,1,0:T(8,128)}, u32[]{:S(2)}, u32[]{:S(2)}) %all-to-all-start.2) | async-done | bytes 1572896 | tf_op jit(solution)/shard_map/all_to_all | solution.py:44
  132.2 13.0 %scatter_custom_fusion.1 = f32[1024,192]{1,0:T(8,128)} fusion(s32[2048]{0:T(1024)S(1)} %reshape.208, f32[2048,192]{1,0:T(8,128)} %bitcast.13, f32[]{:T(128)} %constant.41.clone.1), kind=kCustom, calls=%fused_computation.17 | custom fusion | flops 393216 | bytes 786944 | tf_op jit(solution)/shard_map/scatter-add | solution.py:47
  145.6 1.5 reshape.176
  147.1 0.4 fusion
  147.5 0.5 copy.37
  148.0 2.0 reshape.177
  150.0 410.6 %all-reduce.5.cloned.1.call-done = f32[256,256]{0,1:T(8,128)} async-done(((f32[256,256]{0,1:T(8,128)}), f32[256,256]{0,1:T(8,128)}) %all-reduce.5.cloned.1.call-update) | async-done | bytes 262160 | tf_op jit(solution)/shard_map/psum | solution.py:49
  560.6 1.0 broadcast_multiply_fusion
  561.6 0.8 copy.44
  562.4 107.0 %all-reduce.3.cloned.1.call-done = f32[1024,192]{1,0:T(8,128)} async-done(((f32[1024,192]{1,0:T(8,128)}), f32[1024,192]{1,0:T(8,128)}) %all-reduce.3.cloned.1.call-update) | async-done | bytes 786448 | tf_op jit(solution)/shard_map/psum | solution.py:48
  669.4 2.4 copy.43
  (33 shorter events, 1.3 us)
Async XLA Ops:
  7.2 41.7 %copy-start = (bf16[256,256]{1,0:T(8,128)(2,1)S(1)}, bf16[256,256]{1,0:T(8,128)(2,1)}, u32[]{:S(2)}) copy-start(bf16[256,256]{1,0:T(8,128)(2,1)} %param.12) | copy-start | bytes 393220
  8.6 24.0 %all-to-all-start = ((s32[1,64,32]{2,0,1:T(1,128)}), s32[1,64,32]{2,0,1:T(1,128)S(1)}, u32[]{:S(2)}, u32[]{:S(2)}) async-start(s32[1,64,32]{2,0,1:T(1,128)} %copy.32), calls=%async_computation | async-start | bytes 65536 | tf_op jit(solution)/shard_map/all_to_all | solution.py:13
  41.5 6.2 copy-start.1
  42.7 6.1 copy-start.4
  42.7 33.0 %all-to-all-start.1 = ((bf16[64,32,192]{2,1,0:T(8,128)(2,1)}), bf16[64,32,192]{2,1,0:T(8,128)(2,1)S(1)}, u32[]{:S(2)}, u32[]{:S(2)}) async-start(bf16[64,32,192]{2,1,0:T(8,128)(2,1)} %broadcast_select_fusion), calls=%async_computation.1 | async-start | bytes 2097152 | tf_op jit(solution)/shard_map/all_to_all | solution.py:16
  50.5 2.8 copy-start.3
  75.8 56.4 %all-to-all-start.2 = ((f32[64,32,192]{2,1,0:T(8,128)}), f32[64,32,192]{2,1,0:T(8,128)}, u32[]{:S(2)}, u32[]{:S(2)}) async-start(f32[64,32,192]{2,1,0:T(8,128)} %bitcast.41), calls=%async_computation.2 | async-start | bytes 4194304 | tf_op jit(solution)/shard_map/all_to_all | solution.py:44
  82.4 478.2 %all-reduce.5.cloned.1.call-start = ((), (), s32[]{:S(2)}) async-start(), calls=%async_computation.4 | async-start | bytes 524288 | tf_op jit(solution)/shard_map/psum | solution.py:49
  92.0 2.1 copy-start.5
  92.7 1.5 copy-start.2
  94.0 575.5 %all-reduce.3.cloned.1.call-start = ((), (), s32[]{:S(2)}) async-start(), calls=%async_computation.3 | async-start | bytes 2097152 | tf_op jit(solution)/shard_map/psum | solution.py:48
Sparse Core Ops, SparseCore 0:
  94.1 466.4 all-reduce.4
  563.1 106.2 all-reduce.2
where the time goes:
time: 685 us; the launch traced here: 679 us
  waiting for transfers between devices  574 us (84%)
  local copies, waits for them, and re-layouts  42.1 us (6%)
  starting transfers between devices  26.3 us (4%)
  other arithmetic  17.8 us (3%)
  between operations  14.3 us (2%)
    psum x1, waiting for transfers between devices, on_device(): weight_total = lax.psum(weight_local, ('dp', 'emb'))  411 us
    psum x1, waiting for transfers between devices, on_device(): table_grad = lax.psum(table_local, 'dp')  107 us
    all_to_all x1, waiting for transfers between devices, on_device(): lax.all_to_all(ordered.reshape(groups, -1, width), 'emb', split_axis=0, c...  36.9 us
    all_to_all x1, starting transfers between devices, on_device(): lax.all_to_all(requests, 'emb', split_axis=1, concat_axis=1, tiled=True)  14.5 us
  transfers between devices with their start and end apart: 5, of which 5 were waited for; matrix products, arithmetic and copies ran while one was open for 7% of the time, Pallas kernels for 0%

commit v1 on v0

v1 whole, which is shorter than its diff:
```python
import functools

import jax
import jax.numpy as jnp
from jax import lax
from jax.experimental import pallas as pl
from jax.experimental.pallas import tpu as pltpu
from jax.sharding import PartitionSpec as P

MESH = pl.DeviceIdType.MESH
BF = jnp.bfloat16
F32 = jnp.float32
NZ, NY, NX, NC = 12, 8, 4, 2
NP = NY * NX * NC
D, NTOK, RANK, NCOMP, B, ROWS, CAP = 192, 256, 96, 256, 8, 1024, 32
TOK = B * NTOK
PACK = CAP + CAP // 2
SAMPLES = 6144


def dot(a, b):
    return jnp.dot(a, b, preferred_element_type=F32)


def dot_t(a, b):
    return lax.dot_general(a, b, (((1,), (1,)), ((), ())), preferred_element_type=F32)


def onehot(mask):
    return mask.astype(F32).astype(BF)


def alternate(e, n):
    half = (e + 1) // 2
    return lax.rem(jnp.where(lax.rem(e, 2) == 1, half, n - half), n)


def kernel(
    table_t, req_t, slot, mask, proj_t, weight, cot,
    fm_o, comp_o, tg_o, wg_o,
    reqs, reqr, wrow, wcol, slot8, smcol,
    cplane, cb, rg, table, wt,
    bsend, brecv, asend, arecv, ret, arr,
    tgf, zsend, zrecv, zfull,
    weo, bdp, bdc, fplane, mplane,
    wsum, wrecv, wtile, wzrecv, wfin, wfull,
    s_rq, s_b, s_a, s_z, s_w, s_wz, s_wg, s_gs, s_gr,
):
    z = lax.axis_index("dp")
    me = lax.axis_index("emb")
    my = me // (NX * NC)
    mx = lax.rem(me // NC, NX)
    mc = lax.rem(me, NC)

    def peer(j):
        dy = alternate(lax.rem(j, NY), NY)
        dxc = j // NY
        py = lax.rem(my + dy, NY)
        px = lax.rem(mx + dxc // NC, NX)
        pc = lax.rem(mc + dxc, NC)
        return (py * NX + px) * NC + pc

    def zpeer(j):
        return lax.rem(z + alternate(j, NZ), NZ)

    def wait(ref, sem):
        pltpu.make_async_copy(ref, ref, sem).wait()

    def plane_send(src, dst, sems):
        def body(j, carry):
            p = peer(j)
            pltpu.make_async_remote_copy(
                src_ref=src(p), dst_ref=dst, send_sem=sems.at[0], recv_sem=sems.at[1],
                device_id={"emb": p}, device_id_type=MESH,
            ).start()
            return carry
        lax.fori_loop(1, NP, body, 0)

    def z_send(src, dst, sems):
        def body(j, carry):
            p = zpeer(j)
            pltpu.make_async_remote_copy(
                src_ref=src(p), dst_ref=dst, send_sem=sems.at[0], recv_sem=sems.at[1],
                device_id={"dp": p}, device_id_type=MESH,
            ).start()
            return carry
        lax.fori_loop(1, NZ, body, 0)

    barrier = pltpu.get_barrier_semaphore()

    def sig_plane(j, carry):
        pl.semaphore_signal(barrier, inc=1, device_id={"emb": peer(j)}, device_id_type=MESH)
        return carry

    def sig_z(j, carry):
        pl.semaphore_signal(barrier, inc=1, device_id={"dp": zpeer(j)}, device_id_type=MESH)
        return carry

    lax.fori_loop(1, NP, sig_plane, 0)
    lax.fori_loop(1, NZ, sig_z, 0)

    lane = lax.broadcasted_iota(jnp.int32, (1, 128), 1)
    low = lane < 64

    rt = jnp.concatenate([req_t[...], jnp.zeros((128 - CAP, NP), jnp.int32)], 0)
    rt = jnp.concatenate([rt, jnp.zeros((128, 128 - NP), jnp.int32)], 1).T
    rt = rt[0:NP]
    tiled = rt
    for i in range(1, 4):
        tiled = tiled + pltpu.roll(rt, 32 * i, 1)
    tiled = jnp.where(lane // CAP == lax.rem(me, 4), tiled, 0)
    for p in range(NP):
        reqs[p] = tiled[p : p + 1]
    reqr[lax.rem(me, 4) * 16 + me // 4] = reqs[me]

    for b in range(B):
        slot8[b : b + 1, :] = slot[0:1, b * NTOK : (b + 1) * NTOK]
    masked = jnp.where(mask[...] > 0, slot8[...], -1)
    slot8[...] = masked
    smcol[...] = jnp.concatenate([masked, jnp.full((120, NTOK), -1, jnp.int32)], 0).T

    pl.semaphore_wait(barrier, NP - 1 + NZ - 1)
    plane_send(lambda p: reqs.at[p], reqr.at[lax.rem(me, 4) * 16 + me // 4], s_rq)

    def unpack_cot(mp, carry):
        at = pl.multiple_of(mp * 384, 128)
        x = cot[:, pl.ds(at, 384)].astype(F32)
        x0, x1, x2 = x[:, 0:128], x[:, 128:256], x[:, 256:384]
        r1 = pltpu.roll(x1, 64, 1)
        r2 = pltpu.roll(x2, 64, 1)
        ev, od = pl.ds(2 * mp, B, stride=NCOMP), pl.ds(2 * mp + 1, B, stride=NCOMP)
        cplane[0, ev, :] = x0
        cplane[1, ev, :] = jnp.where(low, x1, r1)
        cplane[0, od, :] = jnp.where(low, r1, r2)
        cplane[1, od, :] = jnp.where(low, r2, x2)
        return carry

    lax.fori_loop(0, NCOMP // 2, unpack_cot, 0, unroll=8)
    wt[...] = weight[...].astype(F32).T.astype(BF)

    def make_rg(b, carry):
        rows = pl.ds(pl.multiple_of(b * NCOMP, NCOMP), NCOMP)
        c = jnp.concatenate([cplane[0, rows, :], cplane[1, rows, :]], 1).astype(BF)
        cb[rows, :] = c
        rg[rows, :] = dot(wt[...], c).astype(BF)
        return carry

    lax.fori_loop(0, B, make_rg, 0)

    sub = lax.broadcasted_iota(jnp.int32, (128, 1), 0)

    def packed(val, dst, g):
        for q in range(4):
            v = val[q * CAP : (q + 1) * CAP]
            dst[g * 4 + q, 0:CAP, :] = v[:, 0:128].astype(BF)
            dst[g * 4 + q, CAP:PACK, :] = jnp.where(low, v[0:16, 128:256], v[16:32, 128:256]).astype(BF)

    def order(e, carry):
        g = lax.rem(me // 4 + alternate(e, 16), 16)
        key = sub + g * 128
        pt = jnp.concatenate([onehot(slot8[b : b + 1, :] == key) for b in range(B)], 1)
        packed(dot(pt, rg[...]), bsend, g)
        return carry

    lax.fori_loop(0, 16, order, 0)
    brecv[me] = bsend[me]
    plane_send(lambda p: bsend.at[p], brecv.at[me], s_b)

    for i in range(8):
        blk = table_t[:, i * 128 : (i + 1) * 128].astype(F32)
        blk = jnp.concatenate([blk, blk[128:192]], 0).T
        table[i * 128 : (i + 1) * 128, :] = blk.astype(BF)

    wait(reqr.at[pl.ds(0, NP - 1)], s_rq.at[1])
    for g in range(16):
        wrow[g : g + 1, :] = reqr[g] + reqr[16 + g] + reqr[32 + g] + reqr[48 + g]
    wc = jnp.concatenate([wrow[...], jnp.zeros((112, 128), jnp.int32)], 0).T
    for g in range(16):
        wcol[g] = jnp.broadcast_to(wc[:, g : g + 1], (128, 128))
    rlane = lax.broadcasted_iota(jnp.int32, (1, 128), 1)

    def fetch(e, carry):
        g = lax.rem(me // 4 + alternate(e, 16), 16)
        col = wcol[g]
        o = jnp.concatenate([onehot(col == rlane + 128 * i) for i in range(8)], 1)
        packed(dot(o, table[...]), asend, g)
        return carry

    lax.fori_loop(0, 16, fetch, 0)
    arecv[me] = asend[me]
    plane_send(lambda p: asend.at[p], arecv.at[me], s_a)

    def unpack(src, dst):
        def body(p, carry):
            at = pl.multiple_of(p * CAP, CAP)
            dst[pl.ds(at, CAP), 0:128] = src[p, 0:CAP, :]
            h = src[p, CAP:PACK, :].astype(F32)
            dst[pl.ds(at, 16), 128:256] = jnp.where(low, h, 0.0).astype(BF)
            h = pltpu.roll(h, 64, 1)
            dst[pl.ds(pl.multiple_of(at + 16, 16), 16), 128:256] = jnp.where(low, h, 0.0).astype(BF)
            return carry
        lax.fori_loop(0, NP, body, 0, unroll=4)

    wait(brecv.at[pl.ds(0, NP - 1)], s_b.at[1])
    unpack(brecv, ret)

    def scatter(rb, carry):
        key = sub + rb * 128
        o = jnp.concatenate([onehot(wrow[g : g + 1, :] == key) for g in range(16)], 1)
        t = dot(o, ret[...])
        t = t.T[0:D].reshape(NZ, 16, 128)
        at = pl.ds(pl.multiple_of(rb * 128, 128), 128)
        tgf[:, :, at] = t
        zsend[:, :, at] = t.astype(BF)
        return carry

    lax.fori_loop(0, 8, scatter, 0)
    z_send(lambda p: zsend.at[p], zrecv.at[z], s_z)

    r256 = lax.broadcasted_iota(jnp.int32, (256, 256), 0)
    c256 = lax.broadcasted_iota(jnp.int32, (256, 256), 1)
    q_fm = onehot(c256 == 4 * lax.rem(r256, 64) + r256 // 64)
    q_w = onehot(c256 == 2 * lax.rem(r256, 128) + r256 // 128)
    wp = dot(q_w, weight[...]).astype(BF)
    weo[...] = jnp.concatenate([wp[0:128], wp[128:256]], 1)
    bdp[...] = jnp.zeros_like(bdp)
    bdc[...] = jnp.zeros_like(bdc)
    zlane = lax.broadcasted_iota(jnp.int32, (1, TOK), 1)

    wait(arecv.at[pl.ds(0, NP - 1)], s_a.at[1])
    unpack(arecv, arr)
    wsum[...] = jnp.zeros_like(wsum)
    colid = lax.broadcasted_iota(jnp.int32, (NTOK, 128), 1)

    def forward(b, carry):
        rows = pl.ds(pl.multiple_of(b * NTOK, NTOK), NTOK)
        key = jnp.sum(jnp.where(colid == b, smcol[...], 0), axis=1, keepdims=True)
        ef = dot(onehot(key == zlane), arr[...])
        e = ef.astype(BF)
        wsum[...] += dot_t(cb[rows, :], e)
        pj = dot(proj_t[...], e).astype(BF)
        for i in range(4):
            bdp[i * RANK : (i + 1) * RANK, i * 256 : (i + 1) * 256] = pj
        ep = dot(q_fm, e).astype(BF)
        ecat = jnp.concatenate([ep[i * 64 : (i + 1) * 64] for i in range(4)], 1)
        x = dot_t(ecat, bdp[...])
        mean = jnp.sum(x, keepdims=True) / (NTOK * RANK)
        xc = x - mean
        var = jnp.sum(xc * xc, keepdims=True) / (NTOK * RANK)
        xn = xc * lax.rsqrt(var + 1e-05)
        for i in range(3):
            fplane[i, pl.ds(pl.multiple_of(b * 64, 64), 64), :] = xn[:, i * 128 : (i + 1) * 128]
        ra, rb = pltpu.roll(ef[:, 0:128], 64, 1), pltpu.roll(ef[:, 128:256], 64, 1)
        bdc[0:256, 0:256] = e
        bdc[256:512, 128:256] = jnp.where(low, 0.0, ra).astype(BF)
        bdc[256:512, 256:384] = jnp.where(low, ra, rb).astype(BF)
        y = dot(weo[...], bdc[...])
        for i in range(3):
            mplane[i, pl.ds(pl.multiple_of(b * 128, 128), 128), :] = y[:, i * 128 : (i + 1) * 128]
        return carry

    lax.fori_loop(0, B, forward, 0)

    def wtile_at(ref, p):
        return ref.at[pl.ds(pl.multiple_of((p // 2) * 8, 8), 8), pl.ds(pl.multiple_of(lax.rem(p, 2) * 128, 128), 128)]

    wrecv[me] = wtile_at(wsum, me)[...]
    plane_send(lambda p: wtile_at(wsum, p), wrecv.at[me], s_w)

    wait(zrecv.at[pl.ds(0, NZ - 1)], s_z.at[1])
    zrecv[z] = jnp.zeros((16, ROWS), BF)
    acc = tgf[z]
    for i in range(NZ):
        acc = acc + zrecv[i].astype(F32)
    zfull[z] = acc

    def ring(s, way):
        k = 2 * s + way
        if way == 0:
            c, to = lax.rem(z - s + NZ, NZ), lax.rem(z + 1, NZ)
        else:
            c, to = lax.rem(z + s, NZ), lax.rem(z + NZ - 1, NZ)
        return pltpu.make_async_remote_copy(
            src_ref=zfull.at[c], dst_ref=zfull.at[c], send_sem=s_gs.at[k], recv_sem=s_gr.at[k],
            device_id={"dp": to}, device_id_type=MESH,
        )

    def ring_recv(s, way):
        c = lax.rem(z - s - 1 + NZ, NZ) if way == 0 else lax.rem(z + s + 1, NZ)
        pltpu.make_async_copy(zfull.at[c], zfull.at[c], s_gr.at[2 * s + way]).wait()

    ring(0, 0).start()
    ring(0, 1).start()

    def out_fm(q, carry):
        for i in range(3):
            at = pl.multiple_of(q * 384 + i * 128, 128)
            fm_o[:, pl.ds(at, 128)] = fplane[i, pl.ds(q, B, stride=64), :].astype(BF)
        return carry

    lax.fori_loop(0, 64, out_fm, 0, unroll=8)

    def out_comp(q, carry):
        for i in range(3):
            at = pl.multiple_of(q * 384 + i * 128, 128)
            comp_o[:, pl.ds(at, 128)] = mplane[i, pl.ds(q, B, stride=128), :].astype(BF)
        return carry

    lax.fori_loop(0, 128, out_comp, 0, unroll=8)

    wait(wrecv.at[pl.ds(0, NP - 1)], s_w.at[1])
    wtile[...] = jnp.sum(wrecv[...], axis=0)
    wzrecv[z] = wtile[...]
    z_send(lambda p: wtile, wzrecv.at[z], s_wz)

    ring_recv(0, 0)
    ring(1, 0).start()
    ring_recv(0, 1)
    ring(1, 1).start()

    wait(wzrecv.at[pl.ds(0, NZ - 1)], s_wz.at[1])
    wfin[...] = jnp.sum(wzrecv[...], axis=0) / SAMPLES
    wtile_at(wfull, me)[...] = wfin[...]
    plane_send(lambda p: wfin, wtile_at(wfull, me), s_wg)

    for s in range(1, 6):
        ring_recv(s, 0)
        if s < 5:
            ring(s + 1, 0).start()
            ring_recv(s, 1)
            if s < 4:
                ring(s + 1, 1).start()
    tg_o[...] = zfull[...].reshape(D, ROWS)

    wait(wrecv.at[pl.ds(0, NP - 1)], s_wg.at[1])
    wg_o[...] = wfull[...]

    wait(reqs.at[pl.ds(0, NP - 1)], s_rq.at[0])
    wait(bsend.at[pl.ds(0, NP - 1)], s_b.at[0])
    wait(asend.at[pl.ds(0, NP - 1)], s_a.at[0])
    wait(zsend.at[pl.ds(0, NZ - 1)], s_z.at[0])
    wait(wrecv.at[pl.ds(0, NP - 1)], s_w.at[0])
    wait(wzrecv.at[pl.ds(0, NZ - 1)], s_wz.at[0])
    wait(wrecv.at[pl.ds(0, NP - 1)], s_wg.at[0])
    for s in range(6):
        ring(s, 0).wait_send()
        if s < 5:
            ring(s, 1).wait_send()


def on_device(emb_table, requests, token_slot, kept_mask, fm_proj, comp_weight, comp_cotangent):
    vm = pl.BlockSpec(memory_space=pltpu.VMEM)
    v = pltpu.VMEM
    dma2 = pltpu.SemaphoreType.DMA((2,))
    fm, comp, tg_t, wg = pl.pallas_call(
        kernel,
        out_shape=(
            jax.ShapeDtypeStruct((B, NTOK * RANK), BF),
            jax.ShapeDtypeStruct((B, NCOMP * D), BF),
            jax.ShapeDtypeStruct((D, ROWS), F32),
            jax.ShapeDtypeStruct((NCOMP, NTOK), F32),
        ),
        in_specs=[vm] * 7,
        out_specs=(vm,) * 4,
        scratch_shapes=[
            v((NP, 1, 128), jnp.int32), v((NP, 1, 128), jnp.int32),
            v((16, 128), jnp.int32), v((16, 128, 128), jnp.int32),
            v((B, NTOK), jnp.int32), v((NTOK, 128), jnp.int32),
            v((2, TOK, 128), F32), v((TOK, 256), BF), v((TOK, 256), BF),
            v((ROWS, 256), BF), v((256, 256), BF),
            v((NP, PACK, 128), BF), v((NP, PACK, 128), BF),
            v((NP, PACK, 128), BF), v((NP, PACK, 128), BF),
            v((TOK, 256), BF), v((TOK, 256), BF),
            v((NZ, 16, ROWS), F32), v((NZ, 16, ROWS), BF),
            v((NZ, 16, ROWS), BF), v((NZ, 16, ROWS), F32),
            v((128, 512), BF), v((384, 1024), BF), v((512, 384), BF),
            v((3, 512, 128), F32), v((3, 1024, 128), F32),
            v((256, 256), F32), v((NP, 8, 128), F32), v((8, 128), F32),
            v((NZ, 8, 128), F32), v((8, 128), F32), v((256, 256), F32),
            dma2, dma2, dma2, dma2, dma2, dma2, dma2,
            pltpu.SemaphoreType.DMA((12,)), pltpu.SemaphoreType.DMA((12,)),
        ],
        compiler_params=pltpu.CompilerParams(
            collective_id=0, has_side_effects=True, vmem_limit_bytes=48 * 1024 * 1024
        ),
    )(
        emb_table.T, requests[0].T, token_slot, kept_mask, fm_proj.T, comp_weight, comp_cotangent
    )
    return fm, comp, tg_t.T, wg


def solution(mesh):
    return jax.shard_map(
        on_device,
        mesh=mesh,
        in_specs=(
            P("emb", None),
            P(("dp", "emb"), None, None),
            P(("dp", "emb"), None),
            P(("dp", "emb"), None),
            P(),
            P(),
            P(("dp", "emb"), None),
        ),
        out_specs=(P(("dp", "emb"), None), P(("dp", "emb"), None), P("emb", None), P()),
        check_vma=False,
    )
```

time: 685 us -> 126 us (0.18)
  the two profiles are of different devices: /device:TPU:1 before, /device:TPU:16 now
where the time goes in v1:
time: 126 us
  Pallas kernels  116 us (92%)
  local copies, waits for them, and re-layouts  9.14 us (7%)
    pallas_call x1, Pallas kernels, on_device(): pl.pallas_call(kernel, out_shape=(jax.ShapeDtypeStruct((B, NTOK * RANK),...  116 us
    unnamed x18, local copies, waits for them, and re-layouts  9.14 us

profile of v1, /device:TPU:16, one launch (start us, length us, event | category | flops | bytes accessed | tf_op | source)
XLA Modules:
  0.0 125.7 jit_solution(1926568178801573391)
XLA Ops:
  0.6 0.0 copy-start
  0.6 1.1 copy-done
  1.8 0.0 copy-start.1
  1.8 1.0 copy-done.1
  2.8 0.0 copy-start.2
  2.8 0.9 copy-done.2
  3.7 0.0 copy-start.3
  3.7 0.8 copy-done.3
  4.5 0.0 copy-start.4
  4.5 0.7 copy-done.4
  5.2 0.0 copy-start.5
  5.2 0.7 copy-done.5
  5.9 0.0 copy-start.6
  5.9 0.7 copy-done.6
  6.6 115.9 %shard_map.102 = (bf16[8,24576]{1,0:T(8,128)(2,1)S(1)}, bf16[8,49152]{1,0:T(8,128)(2,1)S(1)}, f32[192,1024]{1,0:T(8,128)S(1)}, f32[256,256]{1,0:T(8,128)S(1)}) custom-call(bf16[192,1024]{1,0:T(8,128)(2,1)S(1)} %bitcast.7, s32[32,64]{1,0:T(8,128)S(1)} %bitcast.9, s32[1,2048]{1,0:T(1,128)S(1)} %copy-done.5, s32[8,256]{1,0:T(8,128)S(1)} %copy-done.6, ...), custom_call_target="tpu_custom_call" | custom-call | tf_op jit(solution)/shard_map/pallas_call | solution.py:355
  122.5 0.7 copy.15
  123.3 0.9 copy.16
  124.2 0.9 copy.17
  125.0 0.7 copy.18
Async XLA Ops:
  0.6 1.1 copy-start
  1.8 1.0 copy-start.1
  2.8 0.9 copy-start.2
  3.7 0.8 copy-start.3
  4.5 0.7 copy-start.4
  5.2 0.7 copy-start.5
  5.9 0.7 copy-start.6

commit v2 on v1

v2 whole, which is shorter than its diff:
```python
import functools

import jax
import jax.numpy as jnp
from jax import lax
from jax.experimental import pallas as pl
from jax.experimental.pallas import tpu as pltpu
from jax.sharding import PartitionSpec as P

MESH = pl.DeviceIdType.MESH
BF = jnp.bfloat16
F32 = jnp.float32
NZ, NY, NX, NC = 12, 8, 4, 2
NP = NY * NX * NC
D, NTOK, RANK, NCOMP, B, ROWS, CAP = 192, 256, 96, 256, 8, 1024, 32
TOK = B * NTOK
PACK = CAP + CAP // 2
SAMPLES = 6144


def dot(a, b):
    return jnp.dot(a, b, preferred_element_type=F32)


def dot_t(a, b):
    return lax.dot_general(a, b, (((1,), (1,)), ((), ())), preferred_element_type=F32)


def onehot(mask):
    return mask.astype(F32).astype(BF)


def alternate(e, n):
    half = (e + 1) // 2
    return lax.rem(jnp.where(lax.rem(e, 2) == 1, half, n - half), n)


def far_first(e):
    return alternate(15 - e, 16)


def kernel(
    table_h, req_h, slot_h, mask_h, proj_h, weight_h, cot_h,
    fm_h, comp_h, tg_h, wg_h,
    fm_o, comp_o,
    table_t, req_t, slot, mask, proj_t, weight, cot,
    reqs, reqm, reqr, wrow, wcol, slot8, keyb, pq,
    cplane, cb, rg, table, wt,
    bsend, brecv, asend, arecv, ret, arr,
    tgf, zsend, zrecv, zfull,
    eb, weo, bdp, bdc, fplane, mplane,
    wsum, wb, w1, wpart, w2, wtile, wzrecv, wquart, wq, wfull, wg_o, tg_o,
    s_in, s_rq, s_rq2, s_b, s_as, s_ar, s_z, s_w1, s_w2, s_wz, s_w4, s_w5, s_gs, s_gr, s_out,
):
    loads = [
        pltpu.make_async_copy(src, dst, s_in.at[i])
        for i, (src, dst) in enumerate([
            (req_h, req_t), (slot_h, slot), (mask_h, mask), (cot_h, cot),
            (weight_h, weight), (table_h, table_t), (proj_h, proj_t),
        ])
    ]
    for load in loads:
        load.start()
    z = lax.axis_index("dp")
    me = lax.axis_index("emb")
    my = me // (NX * NC)
    mx = lax.rem(me // NC, NX)
    mc = lax.rem(me, NC)

    def peer(j):
        dy = alternate(lax.rem(j, NY), NY)
        dxc = j // NY
        py = lax.rem(my + dy, NY)
        px = lax.rem(mx + dxc // NC, NX)
        pc = lax.rem(mc + dxc, NC)
        return (py * NX + px) * NC + pc

    def zpeer(j):
        return lax.rem(z + alternate(j, NZ), NZ)

    def wait(ref, sem):
        pltpu.make_async_copy(ref, ref, sem).wait()

    mxc = lax.rem(me, NX * NC)

    def row_peer(k):
        return lax.rem(mxc + k, NX * NC)

    def row_send(src, dst, sems):
        for k in range(1, NX * NC):
            xc = row_peer(k)
            pltpu.make_async_remote_copy(
                src_ref=src(xc), dst_ref=dst, send_sem=sems.at[0], recv_sem=sems.at[1],
                device_id={"emb": my * NX * NC + xc}, device_id_type=MESH,
            ).start()

    def column_send(src, dst, sems):
        for k in range(1, NY):
            y = lax.rem(my + alternate(jnp.int32(k), NY), NY)
            pltpu.make_async_remote_copy(
                src_ref=src(y), dst_ref=dst, send_sem=sems.at[0], recv_sem=sems.at[1],
                device_id={"emb": y * NX * NC + mxc}, device_id_type=MESH,
            ).start()

    def z_send(src, dst, sems):
        def body(j, carry):
            p = zpeer(j)
            pltpu.make_async_remote_copy(
                src_ref=src(p), dst_ref=dst, send_sem=sems.at[0], recv_sem=sems.at[1],
                device_id={"dp": p}, device_id_type=MESH,
            ).start()
            return carry
        lax.fori_loop(1, NZ, body, 0)

    barrier = pltpu.get_barrier_semaphore()

    def sig_plane(j, carry):
        pl.semaphore_signal(barrier, inc=1, device_id={"emb": peer(j)}, device_id_type=MESH)
        return carry

    def sig_z(j, carry):
        pl.semaphore_signal(barrier, inc=1, device_id={"dp": zpeer(j)}, device_id_type=MESH)
        return carry

    lax.fori_loop(1, NP, sig_plane, 0, unroll=3)
    lax.fori_loop(1, NZ, sig_z, 0)

    lane = lax.broadcasted_iota(jnp.int32, (1, 128), 1)
    low = lane < 64

    for load in loads[:3]:
        load.wait()

    rt = jnp.concatenate([req_t[...], jnp.zeros((128 - CAP, NP), jnp.int32)], 0)
    rt = jnp.concatenate([rt, jnp.zeros((128, 128 - NP), jnp.int32)], 1).T
    rt = rt[0:NP]
    tiled = rt
    for i in range(1, 4):
        tiled = tiled + pltpu.roll(rt, 32 * i, 1)
    tiled = jnp.where(lane // CAP == lax.rem(me, 4), tiled, 0)
    for p in range(NP):
        reqs[p % 8, p // 8] = tiled[p : p + 1]

    for b in range(B):
        slot8[b : b + 1, :] = slot[0:1, b * NTOK : (b + 1) * NTOK]
    masked = jnp.where(mask[...] > 0, slot8[...], -1)
    slot8[...] = masked

    loads[3].wait()
    loads[4].wait()

    def unpack_cot(mp, carry):
        at = pl.multiple_of(mp * 384, 128)
        x = cot[:, pl.ds(at, 384)].astype(F32)
        x0, x1, x2 = x[:, 0:128], x[:, 128:256], x[:, 256:384]
        r1 = pltpu.roll(x1, 64, 1)
        r2 = pltpu.roll(x2, 64, 1)
        ev, od = pl.ds(2 * mp, B, stride=NCOMP), pl.ds(2 * mp + 1, B, stride=NCOMP)
        cplane[0, ev, :] = x0
        cplane[1, ev, :] = jnp.where(low, x1, r1)
        cplane[0, od, :] = jnp.where(low, r1, r2)
        cplane[1, od, :] = jnp.where(low, r2, x2)
        return carry

    lax.fori_loop(0, NCOMP // 2, unpack_cot, 0, unroll=8)
    wt[...] = weight[...].astype(F32).T.astype(BF)

    def make_rg(b, carry):
        rows = pl.ds(pl.multiple_of(b * NCOMP, NCOMP), NCOMP)
        c = jnp.concatenate([cplane[0, rows, :], cplane[1, rows, :]], 1).astype(BF)
        cb[rows, :] = c
        rg[rows, :] = dot(wt[...], c).astype(BF)
        return carry

    lax.fori_loop(0, B, make_rg, 0)

    pl.semaphore_wait(barrier, NP - 1 + NZ - 1)
    reqm[:, mxc] = reqs[mxc]
    row_send(lambda xc: reqs.at[xc], reqm.at[:, mxc], s_rq)

    sub = lax.broadcasted_iota(jnp.int32, (128, 1), 0)

    def send4(buf, dst, g, send_sem, recv_sem):
        for q in range(4):
            p = g * 4 + lax.rem(me + q, 4)

            @pl.when(p != me)
            def _():
                pltpu.make_async_remote_copy(
                    src_ref=buf.at[p], dst_ref=dst, send_sem=send_sem, recv_sem=recv_sem,
                    device_id={"emb": p}, device_id_type=MESH,
                ).start()

    def packed(val, dst, g):
        for q in range(4):
            v = val[q * CAP : (q + 1) * CAP]
            dst[g * 4 + q, 0:CAP, :] = v[:, 0:128].astype(BF)
            dst[g * 4 + q, CAP:PACK, :] = jnp.where(low, v[0:16, 128:256], v[16:32, 128:256]).astype(BF)

    def order(e, carry):
        g = lax.rem(me // 4 + far_first(e), 16)
        key = sub + g * 128
        pt = jnp.concatenate([onehot(slot8[b : b + 1, :] == key) for b in range(B)], 1)
        packed(dot(pt, rg[...]), bsend, g)
        send4(bsend, brecv.at[me], g, s_b.at[0], s_b.at[1])
        return carry

    lax.fori_loop(0, 6, order, 0)
    wait(reqs.at[pl.ds(0, 7)], s_rq.at[1])
    reqr[my] = reqm[my]
    column_send(lambda y: reqm.at[y], reqr.at[my], s_rq2)
    lax.fori_loop(6, 16, order, 0)
    brecv[me] = bsend[me]

    loads[5].wait()
    for i in range(8):
        blk = table_t[:, i * 128 : (i + 1) * 128].astype(F32)
        blk = jnp.concatenate([blk, blk[128:192]], 0).T
        table[i * 128 : (i + 1) * 128, :] = blk.astype(BF)

    wait(reqr.at[pl.ds(0, 7)], s_rq2.at[1])
    for g in range(16):
        y, h = g // 2, (g % 2) * 4
        wrow[g : g + 1, :] = reqr[y, h] + reqr[y, h + 1] + reqr[y, h + 2] + reqr[y, h + 3]
    wc = jnp.concatenate([wrow[...], jnp.zeros((112, 128), jnp.int32)], 0).T
    for g in range(16):
        wcol[g] = jnp.broadcast_to(wc[:, g : g + 1], (128, 128))
    rlane = lax.broadcasted_iota(jnp.int32, (1, 128), 1)

    def fetch(e, carry):
        g = lax.rem(me // 4 + far_first(e), 16)
        col = wcol[g]
        o = jnp.concatenate([onehot(col == rlane + 128 * i) for i in range(8)], 1)
        packed(dot(o, table[...]), asend, g)
        send4(asend, arecv.at[me], g, s_as, s_ar.at[e // 4])
        return carry

    lax.fori_loop(0, 16, fetch, 0)
    arecv[me] = asend[me]

    def group_from(e):
        return lax.rem(me // 4 - far_first(e) + 16, 16)

    km = jnp.concatenate([slot8[...], jnp.full((120, NTOK), -1, jnp.int32)], 0).T
    for b in range(B):
        keyb[b] = jnp.broadcast_to(km[:, b : b + 1], (NTOK, 128))

    def choose(k, carry):
        q, b = k // B, lax.rem(k, B)
        key = keyb[b]
        o = [onehot(key == rlane + 128 * group_from(4 * q + i)) for i in range(4)]
        pq[q, pl.ds(pl.multiple_of(b * NTOK, NTOK), NTOK), :] = jnp.concatenate(o, 1)
        return carry

    lax.fori_loop(0, 4 * B, choose, 0)

    def unpack_one(src, p, dst, at):
        dst[pl.ds(at, CAP), 0:128] = src[p, 0:CAP, :]
        h = src[p, CAP:PACK, :].astype(F32)
        dst[pl.ds(at, 16), 128:256] = jnp.where(low, h, 0.0).astype(BF)
        h = pltpu.roll(h, 64, 1)
        dst[pl.ds(pl.multiple_of(at + 16, 16), 16), 128:256] = jnp.where(low, h, 0.0).astype(BF)

    wait(brecv.at[pl.ds(0, NP - 1)], s_b.at[1])

    def unpack_ret(p, carry):
        unpack_one(brecv, p, ret, pl.multiple_of(p * CAP, CAP))
        return carry

    lax.fori_loop(0, NP, unpack_ret, 0, unroll=4)

    def scatter(rb, carry):
        key = sub + rb * 128
        o = jnp.concatenate([onehot(wrow[g : g + 1, :] == key) for g in range(16)], 1)
        t = dot(o, ret[...])
        t = t.T[0:D].reshape(NZ, 16, 128)
        at = pl.ds(pl.multiple_of(rb * 128, 128), 128)
        tgf[:, :, at] = t
        zsend[:, :, at] = t.astype(BF)
        return carry

    lax.fori_loop(0, 8, scatter, 0)
    z_send(lambda p: zsend.at[p], zrecv.at[z], s_z)

    def zpart(c):
        return zfull.at[pl.ds(pl.multiple_of(lax.rem(c + NZ, NZ) * 16, 16), 16)]

    steps = [
        (0, 6), (0, 3), (0, -3), (0, 1), (0, -1),
        (-3, 1), (-3, -1), (3, 1), (3, -1), (6, 1), (6, -1),
    ]

    def hand(k):
        a, d = steps[k]
        return pltpu.make_async_remote_copy(
            src_ref=zpart(z + a), dst_ref=zpart(z + a), send_sem=s_gs.at[k], recv_sem=s_gr.at[k],
            device_id={"dp": lax.rem(z + d + NZ, NZ)}, device_id_type=MESH,
        )

    def got(k):
        a, d = steps[k]
        wait(zpart(z - d + a), s_gr.at[k])

    def sum_z():
        wait(zrecv.at[pl.ds(0, NZ - 1)], s_z.at[1])
        zrecv[z] = jnp.zeros((16, ROWS), BF)
        acc = tgf[z]
        for i in range(NZ):
            acc = acc + zrecv[i].astype(F32)
        zpart(z)[...] = acc.astype(BF)
        for k in range(5):
            hand(k).start()

    r256 = lax.broadcasted_iota(jnp.int32, (256, 256), 0)
    c256 = lax.broadcasted_iota(jnp.int32, (256, 256), 1)
    q_fm = onehot(c256 == 4 * lax.rem(r256, 64) + r256 // 64)
    q_w = onehot(c256 == 2 * lax.rem(r256, 128) + r256 // 128)
    wp = dot(q_w, weight[...]).astype(BF)
    weo[...] = jnp.concatenate([wp[0:128], wp[128:256]], 1)
    bdp[...] = jnp.zeros_like(bdp)
    bdc[...] = jnp.zeros_like(bdc)
    loads[6].wait()
    wsum[...] = jnp.zeros_like(wsum)

    def batch_rows(b):
        return pl.ds(pl.multiple_of(b * NTOK, NTOK), NTOK)

    for q in range(4):
        wait(arecv.at[pl.ds(0, 15 if q == 3 else 16)], s_ar.at[q])

        def unpack_arr(k, carry):
            i, c = k // 4, lax.rem(k, 4)
            unpack_one(arecv, group_from(4 * q + i) * 4 + c, arr, pl.multiple_of(k * CAP, CAP))
            return carry

        lax.fori_loop(0, 16, unpack_arr, 0, unroll=4)

        def embed(b, carry):
            rows = batch_rows(b)
            e = dot(pq[q, rows, :], arr[...])
            if q > 0:
                e = e + eb[rows, :].astype(F32)
            e = e.astype(BF)
            eb[rows, :] = e
            if q == 3:
                wsum[...] += dot_t(cb[rows, :], e)
            return carry

        lax.fori_loop(0, B, embed, 0)

    def slab(ref, xc):
        return ref.at[pl.ds(pl.multiple_of(xc * 32, 32), 32)]

    def tile(ref, y):
        return ref.at[pl.ds(pl.multiple_of((y // 2) * 8, 8), 8), pl.ds(pl.multiple_of(lax.rem(y, 2) * 128, 128), 128)]

    wb[...] = wsum[...].astype(BF)
    w1[mxc] = slab(wb, mxc)[...]
    row_send(lambda xc: slab(wb, xc), w1.at[mxc], s_w1)
    sum_z()

    def forward(b, carry):
        e = eb[batch_rows(b), :]
        ef = e.astype(F32)
        pj = dot(proj_t[...], e).astype(BF)
        for i in range(4):
            bdp[i * RANK : (i + 1) * RANK, i * 256 : (i + 1) * 256] = pj
        ep = dot(q_fm, e).astype(BF)
        ecat = jnp.concatenate([ep[i * 64 : (i + 1) * 64] for i in range(4)], 1)
        x = dot_t(ecat, bdp[...])
        mean = jnp.sum(x, keepdims=True) / (NTOK * RANK)
        xc = x - mean
        var = jnp.sum(xc * xc, keepdims=True) / (NTOK * RANK)
        xn = xc * lax.rsqrt(var + 1e-05)
        for i in range(3):
            fplane[i, pl.ds(pl.multiple_of(b * 64, 64), 64), :] = xn[:, i * 128 : (i + 1) * 128]
        ra, rb = pltpu.roll(ef[:, 0:128], 64, 1), pltpu.roll(ef[:, 128:256], 64, 1)
        bdc[0:256, 0:256] = e
        bdc[256:512, 128:256] = jnp.where(low, 0.0, ra).astype(BF)
        bdc[256:512, 256:384] = jnp.where(low, ra, rb).astype(BF)
        y = dot(weo[...], bdc[...])
        for i in range(3):
            mplane[i, pl.ds(pl.multiple_of(b * 128, 128), 128), :] = y[:, i * 128 : (i + 1) * 128]
        return carry

    lax.fori_loop(0, 3, forward, 0)
    wait(w1.at[pl.ds(0, 7)], s_w1.at[1])
    wpart[...] = jnp.sum(w1[...].astype(F32), axis=0)
    w2[my] = tile(wpart, my)[...]
    column_send(lambda y: tile(wpart, y), w2.at[my], s_w2)
    got(1)
    hand(5).start()
    hand(6).start()
    got(2)
    hand(7).start()
    hand(8).start()
    wait(w2.at[pl.ds(0, 7)], s_w2.at[1])
    wtile[...] = jnp.sum(w2[...], axis=0)
    wzrecv[z] = wtile[...]
    z_send(lambda p: wtile, wzrecv.at[z], s_wz)
    got(0)
    hand(9).start()
    hand(10).start()
    lax.fori_loop(3, 6, forward, 0)
    wait(wzrecv.at[pl.ds(0, NZ - 1)], s_wz.at[1])
    tile(wquart, my)[...] = jnp.sum(wzrecv[...], axis=0) / SAMPLES
    column_send(lambda y: tile(wquart, my), tile(wquart, my), s_w4)
    lax.fori_loop(6, B, forward, 0)

    def out_fm(q, carry):
        for i in range(3):
            at = pl.multiple_of(q * 384 + i * 128, 128)
            fm_o[:, pl.ds(at, 128)] = fplane[i, pl.ds(q, B, stride=64), :].astype(BF)
        return carry

    lax.fori_loop(0, 64, out_fm, 0, unroll=8)

    store_fm = pltpu.make_async_copy(fm_o, fm_h, s_out.at[0])
    store_fm.start()
    wait(w2.at[pl.ds(0, 7)], s_w4.at[1])
    wq[...] = wquart[...].astype(BF)
    slab(wfull, mxc)[...] = wq[...]
    row_send(lambda xc: wq, slab(wfull, mxc), s_w5)

    def out_comp(q, carry):
        for i in range(3):
            at = pl.multiple_of(q * 384 + i * 128, 128)
            comp_o[:, pl.ds(at, 128)] = mplane[i, pl.ds(q, B, stride=128), :].astype(BF)
        return carry

    lax.fori_loop(0, 128, out_comp, 0, unroll=8)

    store_comp = pltpu.make_async_copy(comp_o, comp_h, s_out.at[1])
    store_comp.start()
    for k in range(3, 11):
        got(k)
    tg_o[...] = zfull[...].astype(F32)
    store_tg = pltpu.make_async_copy(tg_o, tg_h, s_out.at[2])
    store_tg.start()
    wait(w1.at[pl.ds(0, 7)], s_w5.at[1])
    wg_o[...] = wfull[...].astype(F32)
    store_wg = pltpu.make_async_copy(wg_o, wg_h, s_out.at[3])
    store_wg.start()

    wait(reqs.at[pl.ds(0, 7)], s_rq.at[0])
    wait(reqr.at[pl.ds(0, 7)], s_rq2.at[0])
    wait(bsend.at[pl.ds(0, NP - 1)], s_b.at[0])
    wait(asend.at[pl.ds(0, NP - 1)], s_as)
    wait(zsend.at[pl.ds(0, NZ - 1)], s_z.at[0])
    wait(w1.at[pl.ds(0, 7)], s_w1.at[0])
    wait(w2.at[pl.ds(0, 7)], s_w2.at[0])
    wait(wzrecv.at[pl.ds(0, NZ - 1)], s_wz.at[0])
    wait(w2.at[pl.ds(0, 7)], s_w4.at[0])
    wait(w1.at[pl.ds(0, 7)], s_w5.at[0])
    for k in range(11):
        hand(k).wait_send()
    store_fm.wait()
    store_comp.wait()
    store_tg.wait()
    store_wg.wait()


def deliver(fm_i, comp_i, tg_i, wg_i, fm_o, comp_o, tg_o, wg_o, fm_v, comp_v, tg_v, wg_v, sems):
    held = [(comp_i, comp_v, comp_o), (tg_i, tg_v, tg_o), (fm_i, fm_v, fm_o), (wg_i, wg_v, wg_o)]
    loads = [pltpu.make_async_copy(src, mid, sems.at[0, i]) for i, (src, mid, _) in enumerate(held)]
    stores = [pltpu.make_async_copy(mid, dst, sems.at[1, i]) for i, (_, mid, dst) in enumerate(held)]
    for load in loads:
        load.start()
    for load, store in zip(loads, stores):
        load.wait()
        store.start()
    for store in stores:
        store.wait()


def on_device(emb_table, requests, token_slot, kept_mask, fm_proj, comp_weight, comp_cotangent):
    shapes = (
        jax.ShapeDtypeStruct((B, NTOK * RANK), BF),
        jax.ShapeDtypeStruct((B, NCOMP * D), BF),
        jax.ShapeDtypeStruct((D, ROWS), F32),
        jax.ShapeDtypeStruct((NCOMP, NTOK), F32),
    )
    hbm = pl.BlockSpec(memory_space=pl.ANY)
    v = pltpu.VMEM
    dma2 = pltpu.SemaphoreType.DMA((2,))
    outs = pl.pallas_call(
        kernel,
        out_shape=shapes,
        in_specs=[hbm] * 7,
        out_specs=(hbm,) * 4,
        scratch_shapes=[
            v((B, NTOK * RANK), BF), v((B, NCOMP * D), BF),
            v((D, ROWS), BF), v((CAP, NP), jnp.int32), v((1, TOK), jnp.int32), v((B, NTOK), jnp.int32),
            v((RANK, NTOK), BF), v((NCOMP, NTOK), BF), v((B, NCOMP * D), BF),
            v((8, 8, 1, 128), jnp.int32), v((8, 8, 1, 128), jnp.int32), v((8, 8, 1, 128), jnp.int32),
            v((16, 128), jnp.int32), v((16, 128, 128), jnp.int32),
            v((B, NTOK), jnp.int32), v((B, NTOK, 128), jnp.int32), v((4, TOK, 512), BF),
            v((2, TOK, 128), F32), v((TOK, 256), BF), v((TOK, 256), BF),
            v((ROWS, 256), BF), v((256, 256), BF),
            v((NP, PACK, 128), BF), v((NP, PACK, 128), BF),
            v((NP, PACK, 128), BF), v((NP, PACK, 128), BF),
            v((TOK, 256), BF), v((512, 256), BF),
            v((NZ, 16, ROWS), F32), v((NZ, 16, ROWS), BF),
            v((NZ, 16, ROWS), BF), v((D, ROWS), BF),
            v((TOK, 256), BF), v((128, 512), BF), v((384, 1024), BF), v((512, 384), BF),
            v((3, 512, 128), F32), v((3, 1024, 128), F32),
            v((256, 256), F32), v((256, 256), BF), v((8, 32, 256), BF), v((32, 256), F32), v((8, 8, 128), F32),
            v((8, 128), F32), v((NZ, 8, 128), F32), v((32, 256), F32), v((32, 256), BF), v((256, 256), BF),
            v((NCOMP, NTOK), F32), v((D, ROWS), F32),
            pltpu.SemaphoreType.DMA((7,)), dma2, dma2, dma2, pltpu.SemaphoreType.DMA, pltpu.SemaphoreType.DMA((4,)),
            dma2, dma2, dma2, dma2, dma2, dma2,
            pltpu.SemaphoreType.DMA((12,)), pltpu.SemaphoreType.DMA((12,)), pltpu.SemaphoreType.DMA((4,)),
        ],
        compiler_params=pltpu.CompilerParams(
            collective_id=0, has_side_effects=True, vmem_limit_bytes=62 * 1024 * 1024
        ),
    )(
        emb_table.T, requests[0].T, token_slot, kept_mask, fm_proj.T, comp_weight, comp_cotangent
    )
    fm, comp, tg_t, wg = pl.pallas_call(
        deliver,
        out_shape=shapes,
        in_specs=[hbm] * 4,
        out_specs=(hbm,) * 4,
        scratch_shapes=[v(x.shape, x.dtype) for x in shapes] + [pltpu.SemaphoreType.DMA((2, 4))],
        compiler_params=pltpu.CompilerParams(vmem_limit_bytes=62 * 1024 * 1024),
    )(*outs)
    return fm, comp, tg_t.T, wg


def solution(mesh):
    return jax.shard_map(
        on_device,
        mesh=mesh,
        in_specs=(
            P("emb", None),
            P(("dp", "emb"), None, None),
            P(("dp", "emb"), None),
            P(("dp", "emb"), None),
            P(),
            P(),
            P(("dp", "emb"), None),
        ),
        out_specs=(P(("dp", "emb"), None), P(("dp", "emb"), None), P("emb", None), P()),
        check_vma=False,
    )
```

time: 126 us -> 95.6 us (0.76)
  the two profiles are of different devices: /device:TPU:16 before, /device:TPU:1 now
where the time goes in v2:
time: 95.6 us; the launch traced here: 95.5 us
  Pallas kernels  94.8 us (99%)
    pallas_call x1, Pallas kernels, on_device(): pl.pallas_call(kernel, out_shape=shapes, in_specs=[hbm] * 7, out_specs=(h...  92.3 us
    pallas_call x1, Pallas kernels, on_device(): pl.pallas_call(deliver, out_shape=shapes, in_specs=[hbm] * 4, out_specs=(...  2.55 us

profile of v2, /device:TPU:1, one launch (start us, length us, event | category | flops | bytes accessed | tf_op | source)
XLA Modules:
  0.0 95.5 jit_solution(13917267543290419168)
XLA Ops:
  0.6 92.3 %shard_map.102 = (bf16[8,24576]{1,0:T(8,128)(2,1)}, bf16[8,49152]{1,0:T(8,128)(2,1)}, f32[192,1024]{1,0:T(8,128)}, f32[256,256]{1,0:T(8,128)}) custom-call(bf16[192,1024]{1,0:T(8,128)(2,1)} %bitcast.6, s32[32,64]{1,0:T(8,128)} %bitcast.8, s32[1,2048]{1,0:T(1,128)} %slot_h.1, s32[8,256]{1,0:T(8,128)} %mask_h.1, bf16[96,256]{1,0:T(8,128)(2,1)} %bitcast.7, ...), custom_call_target="tpu_custom_call" | custom-call | tf_op jit(solution)/shard_map/pallas_call | solution.py:486
  92.9 2.6 %shard_map.103 = (bf16[8,24576]{1,0:T(8,128)(2,1)}, bf16[8,49152]{1,0:T(8,128)(2,1)}, f32[192,1024]{1,0:T(8,128)}, f32[256,256]{1,0:T(8,128)}) custom-call(bf16[8,24576]{1,0:T(8,128)(2,1)} %get-tuple-element.12.fm_i, bf16[8,49152]{1,0:T(8,128)(2,1)} %get-tuple-element.13.comp_i, f32[192,1024]{1,0:T(8,128)} %get-tuple-element.14.tg_i, ...), custom_call_target="tpu_custom_call" | custom-call | tf_op jit(solution)/shard_map/pallas_call | solution.py:520

commit v3 on v2

--- a/solution.py
+++ b/solution.py
@@ -269,18 +269,22 @@
 
     lax.fori_loop(0, NP, unpack_ret, 0, unroll=4)
 
+    sub2 = lax.broadcasted_iota(jnp.int32, (256, 1), 0)
+
     def scatter(rb, carry):
-        key = sub + rb * 128
+        key = sub2 + rb * 256
         o = jnp.concatenate([onehot(wrow[g : g + 1, :] == key) for g in range(16)], 1)
         t = dot(o, ret[...])
-        t = t.T[0:D].reshape(NZ, 16, 128)
-        at = pl.ds(pl.multiple_of(rb * 128, 128), 128)
+        t = t.T[0:D].reshape(NZ, 16, 256)
+        at = pl.ds(pl.multiple_of(rb * 256, 256), 256)
         tgf[:, :, at] = t
         zsend[:, :, at] = t.astype(BF)
         return carry
 
-    lax.fori_loop(0, 8, scatter, 0)
-    z_send(lambda p: zsend.at[p], zrecv.at[z], s_z)
+    for h in range(2):
+        lax.fori_loop(2 * h, 2 * h + 2, scatter, 0)
+        half = pl.ds(512 * h, 512)
+        z_send(lambda p: zsend.at[p, :, half], zrecv.at[z, :, half], s_z)
 
     def zpart(c):
         return zfull.at[pl.ds(pl.multiple_of(lax.rem(c + NZ, NZ) * 16, 16), 16)]
@@ -383,11 +387,12 @@
             mplane[i, pl.ds(pl.multiple_of(b * 128, 128), 128), :] = y[:, i * 128 : (i + 1) * 128]
         return carry
 
-    lax.fori_loop(0, 3, forward, 0)
+    lax.fori_loop(0, 4, forward, 0)
     wait(w1.at[pl.ds(0, 7)], s_w1.at[1])
     wpart[...] = jnp.sum(w1[...].astype(F32), axis=0)
     w2[my] = tile(wpart, my)[...]
     column_send(lambda y: tile(wpart, y), w2.at[my], s_w2)
+    lax.fori_loop(4, 5, forward, 0)
     got(1)
     hand(5).start()
     hand(6).start()
@@ -401,11 +406,10 @@
     got(0)
     hand(9).start()
     hand(10).start()
-    lax.fori_loop(3, 6, forward, 0)
+    lax.fori_loop(5, 8, forward, 0)
     wait(wzrecv.at[pl.ds(0, NZ - 1)], s_wz.at[1])
     tile(wquart, my)[...] = jnp.sum(wzrecv[...], axis=0) / SAMPLES
     column_send(lambda y: tile(wquart, my), tile(wquart, my), s_w4)
-    lax.fori_loop(6, B, forward, 0)
 
     def out_fm(q, carry):
         for i in range(3):

time: 95.6 us -> 96 us (level)
  no operation moved by 1% of the time
where the time goes in v3:
time: 96 us; the launch traced here: 95.8 us
  Pallas kernels  95.1 us (99%)
    pallas_call x1, Pallas kernels, on_device(): pl.pallas_call(kernel, out_shape=shapes, in_specs=[hbm] * 7, out_specs=(h...  92.6 us
    pallas_call x1, Pallas kernels, on_device(): pl.pallas_call(deliver, out_shape=shapes, in_specs=[hbm] * 4, out_specs=(...  2.55 us

profile of v3, /device:TPU:1, one launch (start us, length us, event | category | flops | bytes accessed | tf_op | source)
XLA Modules:
  0.0 95.8 jit_solution(15393599737071639703)
XLA Ops:
  0.6 92.6 %shard_map.102 = (bf16[8,24576]{1,0:T(8,128)(2,1)}, bf16[8,49152]{1,0:T(8,128)(2,1)}, f32[192,1024]{1,0:T(8,128)}, f32[256,256]{1,0:T(8,128)}) custom-call(bf16[192,1024]{1,0:T(8,128)(2,1)} %bitcast.6, s32[32,64]{1,0:T(8,128)} %bitcast.8, s32[1,2048]{1,0:T(1,128)} %slot_h.1, s32[8,256]{1,0:T(8,128)} %mask_h.1, bf16[96,256]{1,0:T(8,128)(2,1)} %bitcast.7, ...), custom_call_target="tpu_custom_call" | custom-call | tf_op jit(solution)/shard_map/pallas_call | solution.py:490
  93.2 2.6 %shard_map.103 = (bf16[8,24576]{1,0:T(8,128)(2,1)}, bf16[8,49152]{1,0:T(8,128)(2,1)}, f32[192,1024]{1,0:T(8,128)}, f32[256,256]{1,0:T(8,128)}) custom-call(bf16[8,24576]{1,0:T(8,128)(2,1)} %get-tuple-element.12.fm_i, bf16[8,49152]{1,0:T(8,128)(2,1)} %get-tuple-element.13.comp_i, f32[192,1024]{1,0:T(8,128)} %get-tuple-element.14.tg_i, ...), custom_call_target="tpu_custom_call" | custom-call | tf_op jit(solution)/shard_map/pallas_call | solution.py:524

commit v4 on v3

--- a/solution.py
+++ b/solution.py
@@ -387,22 +387,22 @@
             mplane[i, pl.ds(pl.multiple_of(b * 128, 128), 128), :] = y[:, i * 128 : (i + 1) * 128]
         return carry
 
-    lax.fori_loop(0, 4, forward, 0)
+    lax.fori_loop(0, 3, forward, 0)
     wait(w1.at[pl.ds(0, 7)], s_w1.at[1])
     wpart[...] = jnp.sum(w1[...].astype(F32), axis=0)
     w2[my] = tile(wpart, my)[...]
     column_send(lambda y: tile(wpart, y), w2.at[my], s_w2)
-    lax.fori_loop(4, 5, forward, 0)
+    lax.fori_loop(3, 5, forward, 0)
+    wait(w2.at[pl.ds(0, 7)], s_w2.at[1])
+    wtile[...] = jnp.sum(w2[...], axis=0)
+    wzrecv[z] = wtile[...]
+    z_send(lambda p: wtile, wzrecv.at[z], s_wz)
     got(1)
     hand(5).start()
     hand(6).start()
     got(2)
     hand(7).start()
     hand(8).start()
-    wait(w2.at[pl.ds(0, 7)], s_w2.at[1])
-    wtile[...] = jnp.sum(w2[...], axis=0)
-    wzrecv[z] = wtile[...]
-    z_send(lambda p: wtile, wzrecv.at[z], s_wz)
     got(0)
     hand(9).start()
     hand(10).start()

time: 96 us -> 94.5 us (0.984)
  Pallas kernels: 95.1 us -> 93.7 us
    pallas_call x1, Pallas kernels: 92.6 us -> 91.1 us  [on_device(): pl.pallas_call(kernel, out_shape=shapes, in_specs=[hbm] * 7, out_specs=(h...]
where the time goes in v4:
time: 94.5 us; the launch traced here: 94.3 us
  Pallas kernels  93.7 us (99%)
    pallas_call x1, Pallas kernels, on_device(): pl.pallas_call(kernel, out_shape=shapes, in_specs=[hbm] * 7, out_specs=(h...  91.1 us
    pallas_call x1, Pallas kernels, on_device(): pl.pallas_call(deliver, out_shape=shapes, in_specs=[hbm] * 4, out_specs=(...  2.55 us

profile of v4, /device:TPU:1, one launch (start us, length us, event | category | flops | bytes accessed | tf_op | source)
XLA Modules:
  0.0 94.3 jit_solution(16697379461087109168)
XLA Ops:
  0.6 91.1 %shard_map.102 = (bf16[8,24576]{1,0:T(8,128)(2,1)}, bf16[8,49152]{1,0:T(8,128)(2,1)}, f32[192,1024]{1,0:T(8,128)}, f32[256,256]{1,0:T(8,128)}) custom-call(bf16[192,1024]{1,0:T(8,128)(2,1)} %bitcast.6, s32[32,64]{1,0:T(8,128)} %bitcast.8, s32[1,2048]{1,0:T(1,128)} %slot_h.1, s32[8,256]{1,0:T(8,128)} %mask_h.1, bf16[96,256]{1,0:T(8,128)(2,1)} %bitcast.7, ...), custom_call_target="tpu_custom_call" | custom-call | tf_op jit(solution)/shard_map/pallas_call | solution.py:490
  91.8 2.6 %shard_map.103 = (bf16[8,24576]{1,0:T(8,128)(2,1)}, bf16[8,49152]{1,0:T(8,128)(2,1)}, f32[192,1024]{1,0:T(8,128)}, f32[256,256]{1,0:T(8,128)}) custom-call(bf16[8,24576]{1,0:T(8,128)(2,1)} %get-tuple-element.12.fm_i, bf16[8,49152]{1,0:T(8,128)(2,1)} %get-tuple-element.13.comp_i, f32[192,1024]{1,0:T(8,128)} %get-tuple-element.14.tg_i, ...), custom_call_target="tpu_custom_call" | custom-call | tf_op jit(solution)/shard_map/pallas_call | solution.py:524
